TPU v7x, 32 devices: a whole 2x2x4 slice. The times are simulated.
32 devices in a mesh: grp: 8 (over z, y), shell: 4 (over x, core).
Axes of the slice: x: 2, y: 2, z: 4, core: 2. Of those that a mesh axis runs over, the one named last changes fastest.
Arguments:
- vectors: bfloat16 [8, 4, 384, 256], P('grp', 'shell'), may hold values from -6 to 6
- local_block: bfloat16 [8, 4, 384, 384], P('grp', 'shell'), may hold values from -0.3125 to 0.3125
- pair_blocks: bfloat16 [8, 4, 3, 384, 384], P('grp', 'shell'), may hold values from -0.3125 to 0.3125
- pair_masks: int32 [8, 4, 3, 3, 3], P('grp', 'shell'), may hold values 0 or 1
- shell_block: bfloat16 [8, 4, 384, 384], P('grp', 'shell'), may hold values from -0.3125 to 0.3125
- shell_mask: int32 [8, 4, 3, 3], P('grp', 'shell'), may hold values 0 or 1
- matchings: int32 [3, 8], replicated, may hold values from 0 to 7, as said below
Outputs:
- filtered: bfloat16 [8, 4, 384, 256], P('grp', 'shell')
Inputs may be any that keep to these rules, and one draw needn't show every extreme that they name: Row m of matchings maps every group g to g XOR 2**b_m, for 3 distinct binary digits b_m drawn from the seed.
All inputs are finite; a program needn't handle non-finite values. No bound on the sum of `pair_masks` or of `shell_mask` on one device may be relied on, other than what follows from the above.
Results may differ from a plain program's by a relative error of at most 0.0049.
Values may be sent and summed in bfloat16 or wider, within the bound.
A program may use at most 64 MiB of HBM per device.

v0:
```python
import jax
import jax.numpy as jnp
from jax import lax
from jax.sharding import PartitionSpec as P

BLK = 128


spectrum_center = 1.0
spectrum_halfwidth = 6.0


def from_behind(block, axis, distance):
    devices = range(lax.axis_size(axis))
    route = [(i - distance, i) for i in devices if i - distance in devices]
    return lax.ppermute(block, axis, route)


def from_partner(x, axis, distance):
    return lax.ppermute(x, axis, [(i, i ^ 1 << distance) for i in range(lax.axis_size(axis))])


def widen(mask):
    spread = jnp.repeat(jnp.repeat(mask, BLK, axis=-2), BLK, axis=-1)
    return spread.astype(jnp.bfloat16)


def select_sum(arrays, switches):
    accumulated_rows = jnp.zeros_like(arrays[0])
    for member, switch in zip(arrays, switches):
        accumulated_rows = accumulated_rows + jnp.where(switch, member, jnp.zeros_like(member))
    return accumulated_rows


def transposed(block, current):
    return lax.dot_general(
        block, current, (((0,), (0,)), ((), ())), preferred_element_type=jnp.float32
    )


def on_device(vectors, local_block, pair_blocks, pair_masks, shell_block, shell_mask, matchings):
    initial = vectors[0, 0]
    owned_rows = local_block[0, 0]
    coupled_rows = pair_blocks[0, 0] * widen(pair_masks[0, 0])
    upper_block = shell_block[0, 0] * widen(shell_mask[0, 0])
    matching_total = coupled_rows.shape[0]
    bit_total = lax.axis_size("grp").bit_length() - 1
    group_index = lax.axis_index("grp")
    flip_bits = jnp.bitwise_xor(matchings[:, group_index], group_index)
    chosen = [
        [flip_bits[pairing_index] == 1 << bit_index for bit_index in range(bit_total)]
        for pairing_index in range(matching_total)
    ]

    def operate(current):
        accumulated_rows = jnp.dot(
            owned_rows, current, preferred_element_type=jnp.float32
        ) + transposed(owned_rows, current)
        higher_partner = from_behind(current, "shell", -1)
        accumulated_rows = accumulated_rows + jnp.dot(
            upper_block, higher_partner, preferred_element_type=jnp.float32
        )
        returned = jnp.einsum(
            "mkr,kv->mrv", coupled_rows, current, preferred_element_type=jnp.float32
        ).astype(jnp.bfloat16)
        payload = jnp.stack([jnp.broadcast_to(current, returned.shape), returned], axis=1)
        arrived = []
        for bit_index in range(bit_total):
            outgoing = select_sum(
                [payload[pairing_index] for pairing_index in range(matching_total)],
                [chosen[pairing_index][bit_index] for pairing_index in range(matching_total)],
            )
            arrived.append(from_partner(outgoing, "grp", bit_index))
        received = jnp.stack(
            [select_sum(arrived, chosen[pairing_index]) for pairing_index in range(matching_total)]
        )
        accumulated_rows = accumulated_rows + jnp.einsum(
            "mrk,mkv->rv", coupled_rows, received[:, 0], preferred_element_type=jnp.float32
        )
        accumulated_rows = accumulated_rows + jnp.sum(received[:, 1].astype(jnp.float32), axis=0)
        upward = transposed(upper_block, current).astype(jnp.bfloat16)
        accumulated_rows = accumulated_rows + from_behind(upward, "shell", 1).astype(jnp.float32)
        return accumulated_rows

    current = (
        (operate(initial) - spectrum_center * initial.astype(jnp.float32)) / spectrum_halfwidth
    ).astype(jnp.bfloat16)
    image = operate(current)
    following = 2.0 * (
        image - spectrum_center * current.astype(jnp.float32)
    ) / spectrum_halfwidth - initial.astype(jnp.float32)
    current = following.astype(jnp.bfloat16)
    return current[None, None]


def solution(mesh):
    in_specs = (
        P("grp", "shell", None, None),
        P("grp", "shell", None, None),
        P("grp", "shell", None, None, None),
        P("grp", "shell", None, None, None),
        P("grp", "shell", None, None),
        P("grp", "shell", None, None),
        P(),
    )
    out_specs = P("grp", "shell", None, None)
    return jax.shard_map(
        on_device, mesh=mesh, in_specs=in_specs, out_specs=out_specs, check_vma=False
    )
```

profile of v0, /device:TPU:0, one launch (start us, length us, event | category | flops | bytes accessed | tf_op | source)
XLA Modules:
  0.0 64.6 jit_solution(6662144772430471065)
XLA Ops:
  0.0 1.4 %collective-permute-start = (bf16[384,256]{1,0:T(8,128)(2,1)}, bf16[384,256]{1,0:T(8,128)(2,1)}, u32[]{:S(2)}, u32[]{:S(2)}) collective-permute-start(bf16[384,256]{1,0:T(8,128)(2,1)} %bitcast.152), channel_id=1, source_target_pairs={{1,0},{2,1},{3,2},{5,4},{6,5},{7,6},{9,8},{10,9},{11,10},{13,12},{... | collective-permute-start | bytes 589832 | tf_op jit(solution)/shard_map/ppermute | solution.py:16
  1.4 0.8 %dynamic-slice_xor_fusion = s32[3,1]{1,0:T(4,128)S(1)} fusion(s32[3,8]{1,0:T(4,128)} %param.13, s32[]{:T(128)S(6)} %select_n.203, s32[]{:T(128)S(6)} %axis_index.15), kind=kLoop, calls=%fused_computation.82 | loop fusion | flops 3 | bytes 32 | tf_op jit(solution)/shard_map/xor | solution.py:49
  2.2 0.6 fusion.44
  2.8 2.5 %copy.21 = bf16[1,1,3,384,384]{3,4,2,1,0:T(8,128)(2,1)S(1)} copy(bf16[1,1,3,384,384]{4,3,2,1,0:T(8,128)(2,1)} %param.9) | data formatting | bytes 1769472 | tf_op args[2]
  7.5 0.5 fusion
  8.2 4.1 %collective-permute-start.3 = (bf16[2,384,256]{2,1,0:T(8,128)(2,1)S(1)}, bf16[2,384,256]{2,1,0:T(8,128)(2,1)S(1)}, u32[]{:S(2)}, u32[]{:S(2)}) collective-permute-start(bf16[2,384,256]{2,1,0:T(8,128)(2,1)S(1)} %fusion.20), channel_id=1, source_target_pairs={{0,16},{4,20},{8,24},{12,28},{16,0},{20,4},{24,8},{28,12},{1,17},{... | collective-permute-start | bytes 1179656 | tf_op jit(solution)/shard_map/ppermute | solution.py:20
  16.3 1.6 %collective-permute-start.2 = (bf16[2,384,256]{2,1,0:T(8,128)(2,1)S(1)}, bf16[2,384,256]{2,1,0:T(8,128)(2,1)}, u32[]{:S(2)}, u32[]{:S(2)}) collective-permute-start(bf16[2,384,256]{2,1,0:T(8,128)(2,1)S(1)} %get-tuple-element.14), channel_id=1, source_target_pairs={{0,8},{4,12},{8,0},{12,4},{16,24},{20,28},{24,16},{28,20},{1,9},{5... | collective-permute-start | bytes 1179656 | tf_op jit(solution)/shard_map/ppermute | solution.py:20
  18.0 1.5 %collective-permute-start.1 = (bf16[2,384,256]{2,1,0:T(8,128)(2,1)S(1)}, bf16[2,384,256]{2,1,0:T(8,128)(2,1)}, u32[]{:S(2)}, u32[]{:S(2)}) collective-permute-start(bf16[2,384,256]{2,1,0:T(8,128)(2,1)S(1)} %get-tuple-element.13), channel_id=1, source_target_pairs={{0,4},{4,0},{8,12},{12,8},{16,20},{20,16},{24,28},{28,24},{1,5},{5... | collective-permute-start | bytes 1179656 | tf_op jit(solution)/shard_map/ppermute | solution.py:20
  20.2 2.2 %collective-permute-start.4 = (bf16[384,256]{1,0:T(8,128)(2,1)S(1)}, bf16[384,256]{1,0:T(8,128)(2,1)S(1)}, u32[]{:S(2)}, u32[]{:S(2)}) collective-permute-start(bf16[384,256]{1,0:T(8,128)(2,1)S(1)} %convolution_convert_fusion.3), channel_id=1, source_target_pairs={{0,1},{1,2},{2,3},{4,5},{5,6},{6,7},{8,9},{9,10},{10,11},{12,13},{... | collective-permute-start | bytes 589832 | tf_op jit(solution)/shard_map/ppermute | solution.py:16
  23.2 7.3 %collective-permute-done.3 = bf16[2,384,256]{2,1,0:T(8,128)(2,1)S(1)} collective-permute-done((bf16[2,384,256]{2,1,0:T(8,128)(2,1)S(1)}, bf16[2,384,256]{2,1,0:T(8,128)(2,1)S(1)}, u32[]{:S(2)}, u32[]{:S(2)}) %collective-permute-start.3) | collective-permute-done | bytes 393248 | tf_op jit(solution)/shard_map/ppermute | solution.py:20
  30.4 4.9 %collective-permute-done.2 = bf16[2,384,256]{2,1,0:T(8,128)(2,1)} collective-permute-done((bf16[2,384,256]{2,1,0:T(8,128)(2,1)S(1)}, bf16[2,384,256]{2,1,0:T(8,128)(2,1)}, u32[]{:S(2)}, u32[]{:S(2)}) %collective-permute-start.2) | collective-permute-done | bytes 393248 | tf_op jit(solution)/shard_map/ppermute | solution.py:20
  35.3 1.3 %add_bitcast_fusion.8 = (bf16[1,2,384,256]{3,2,1,0:T(8,128)(2,1)S(1)}, bf16[1,2,384,256]{3,2,1,0:T(8,128)(2,1)S(1)}, bf16[1,2,384,256]{3,2,1,0:T(8,128)(2,1)S(1)}) fusion(bf16[2,384,256]{2,1,0:T(8,128)(2,1)S(1)} %collective-permute-done.3, bf16[2,384,256]{2,1,0:T(8,128)(2,1)} %collective-permute-done.2, bf16[2,384,256]{2,1,0:T(8,128)(2,1)} %collective-permute-done.1, ...), kind=kLoop, calls=%fused_computation.69 | loop fusion | flops 2949120 | bytes 2359305 | tf_op jit(solution)/shard_map/stack | solution.py:74
  36.9 0.5 convolution_bitcast_fusion.1
  37.4 1.3 %fusion.15 = bf16[384,256]{1,0:T(8,128)(2,1)S(1)} fusion(f32[384,256]{1,0:T(8,128)S(1)} %convert_reduce_fusion.1, f32[384,256]{1,0:T(8,128)S(1)} %convolution_bitcast_fusion.1, f32[384,256]{1,0:T(8,128)S(1)} %convolution_add_fusion.3, bf16[384,384]{0,1:T(8,128)(2,1)S(1)} %bitcast_multiply_fusion.1, bf16[384,256]{1,0:T(8,128)(2,1)} %collective-permute-done, ...), kind=kOutput, calls=%fused_computation.37 | convolution fusion | flops 76382208 | bytes 2260992 | tf_op jit(solution)/shard_map/dot_general | solution.py:60
  38.6 0.5 fusion.1
  39.5 1.3 %collective-permute-start.5 = (bf16[384,256]{1,0:T(8,128)(2,1)S(1)}, bf16[384,256]{1,0:T(8,128)(2,1)S(1)}, u32[]{:S(2)}, u32[]{:S(2)}) collective-permute-start(bf16[384,256]{1,0:T(8,128)(2,1)S(1)} %fusion.15), channel_id=1, source_target_pairs={{1,0},{2,1},{3,2},{5,4},{6,5},{7,6},{9,8},{10,9},{11,10},{13,12},{... | collective-permute-start | bytes 589832 | tf_op jit(solution)/shard_map/ppermute | solution.py:16
  41.0 0.7 %collective-permute-start.8 = (bf16[2,384,256]{2,1,0:T(8,128)(2,1)S(1)}, bf16[2,384,256]{2,1,0:T(8,128)(2,1)S(1)}, u32[]{:S(2)}, u32[]{:S(2)}) collective-permute-start(bf16[2,384,256]{2,1,0:T(8,128)(2,1)S(1)} %get-tuple-element.9), channel_id=1, source_target_pairs={{0,16},{4,20},{8,24},{12,28},{16,0},{20,4},{24,8},{28,12},{1,17},{... | collective-permute-start | bytes 1179656 | tf_op jit(solution)/shard_map/ppermute | solution.py:20
  41.8 2.6 %collective-permute-start.7 = (bf16[2,384,256]{2,1,0:T(8,128)(2,1)S(1)}, bf16[2,384,256]{2,1,0:T(8,128)(2,1)S(1)}, u32[]{:S(2)}, u32[]{:S(2)}) collective-permute-start(bf16[2,384,256]{2,1,0:T(8,128)(2,1)S(1)} %add_bitcast_fusion.4), channel_id=1, source_target_pairs={{0,8},{4,12},{8,0},{12,4},{16,24},{20,28},{24,16},{28,20},{1,9},{5... | collective-permute-start | bytes 1179656 | tf_op jit(solution)/shard_map/ppermute | solution.py:20
  44.4 1.5 %collective-permute-start.6 = (bf16[2,384,256]{2,1,0:T(8,128)(2,1)S(1)}, bf16[2,384,256]{2,1,0:T(8,128)(2,1)S(1)}, u32[]{:S(2)}, u32[]{:S(2)}) collective-permute-start(bf16[2,384,256]{2,1,0:T(8,128)(2,1)S(1)} %get-tuple-element.8), channel_id=1, source_target_pairs={{0,4},{4,0},{8,12},{12,8},{16,20},{20,16},{24,28},{28,24},{1,5},{5... | collective-permute-start | bytes 1179656 | tf_op jit(solution)/shard_map/ppermute | solution.py:20
  45.9 2.2 %collective-permute-start.9 = (bf16[384,256]{1,0:T(8,128)(2,1)S(1)}, bf16[384,256]{1,0:T(8,128)(2,1)S(1)}, u32[]{:S(2)}, u32[]{:S(2)}) collective-permute-start(bf16[384,256]{1,0:T(8,128)(2,1)S(1)} %convolution_convert_fusion.2), channel_id=1, source_target_pairs={{0,1},{1,2},{2,3},{4,5},{5,6},{6,7},{8,9},{9,10},{10,11},{12,13},{... | collective-permute-start | bytes 589832 | tf_op jit(solution)/shard_map/ppermute | solution.py:16
  48.1 0.3 fusion.32
  48.7 13.6 %collective-permute-done.8 = bf16[2,384,256]{2,1,0:T(8,128)(2,1)S(1)} collective-permute-done((bf16[2,384,256]{2,1,0:T(8,128)(2,1)S(1)}, bf16[2,384,256]{2,1,0:T(8,128)(2,1)S(1)}, u32[]{:S(2)}, u32[]{:S(2)}) %collective-permute-start.8) | collective-permute-done | bytes 393248 | tf_op jit(solution)/shard_map/ppermute | solution.py:20
  63.0 0.5 convolution_bitcast_fusion
  63.5 1.0 %fusion.16 = bf16[1,1,384,256]{3,2,1,0:T(8,128)(2,1)} fusion(f32[384,256]{1,0:T(8,128)S(1)} %convert_reduce_fusion, f32[384,256]{1,0:T(8,128)S(1)} %convolution_bitcast_fusion, f32[384,256]{1,0:T(8,128)S(1)} %fusion.2, bf16[384,384]{0,1:T(8,128)(2,1)S(1)} %bitcast_multiply_fusion.1, bf16[384,256]{1,0:T(8,128)(2,1)S(1)} %collective-permute-done.5, ...), kind=kOutput, calls=%fused_computation.38 | convolution fusion | flops 76578816 | bytes 2457600 | tf_op jit(solution)/shard_map/dot_general | solution.py:60
  (46 shorter events, 3.8 us)
Async XLA Ops:
  0.0 22.6 %copy-start = (bf16[1,1,384,384]{3,2,1,0:T(8,128)(2,1)S(1)}, bf16[1,1,384,384]{3,2,1,0:T(8,128)(2,1)}, u32[]{:S(2)}) copy-start(bf16[1,1,384,384]{3,2,1,0:T(8,128)(2,1)} %param.8) | copy-start | bytes 884740
  0.0 5.3 %copy-start.3 = (s32[1,1,3,3,3]{4,1,3,2,0:T(1,128)S(1)}, s32[1,1,3,3,3]{4,1,3,2,0:T(1,128)}, u32[]{:S(2)}) copy-start(s32[1,1,3,3,3]{4,1,3,2,0:T(1,128)} %param.10) | copy-start | bytes 328
  0.0 37.3 %collective-permute-start = (bf16[384,256]{1,0:T(8,128)(2,1)}, bf16[384,256]{1,0:T(8,128)(2,1)}, u32[]{:S(2)}, u32[]{:S(2)}) collective-permute-start(bf16[384,256]{1,0:T(8,128)(2,1)} %bitcast.152), channel_id=1, source_target_pairs={{1,0},{2,1},{3,2},{5,4},{6,5},{7,6},{9,8},{10,9},{11,10},{13,12},{... | collective-permute-start | bytes 589832 | tf_op jit(solution)/shard_map/ppermute | solution.py:16
  2.8 4.8 %copy-start.1 = (bf16[1,1,384,256]{3,2,1,0:T(8,128)(2,1)S(1)}, bf16[1,1,384,256]{3,2,1,0:T(8,128)(2,1)}, u32[]{:S(2)}) copy-start(bf16[1,1,384,256]{3,2,1,0:T(8,128)(2,1)} %param.7) | copy-start | bytes 589828
  8.2 11.3 %copy-start.2 = (bf16[1,1,384,384]{3,2,1,0:T(8,128)(2,1)S(1)}, bf16[1,1,384,384]{3,2,1,0:T(8,128)(2,1)}, u32[]{:S(2)}) copy-start(bf16[1,1,384,384]{3,2,1,0:T(8,128)(2,1)} %param.11) | copy-start | bytes 884740
  8.2 22.2 %collective-permute-start.3 = (bf16[2,384,256]{2,1,0:T(8,128)(2,1)S(1)}, bf16[2,384,256]{2,1,0:T(8,128)(2,1)S(1)}, u32[]{:S(2)}, u32[]{:S(2)}) collective-permute-start(bf16[2,384,256]{2,1,0:T(8,128)(2,1)S(1)} %fusion.20), channel_id=1, source_target_pairs={{0,16},{4,20},{8,24},{12,28},{16,0},{20,4},{24,8},{28,12},{1,17},{... | collective-permute-start | bytes 1179656 | tf_op jit(solution)/shard_map/ppermute | solution.py:20
  16.1 3.6 %copy-start.4 = (s32[1,1,3,3]{3,1,2,0:T(1,128)S(1)}, s32[1,1,3,3]{3,1,2,0:T(1,128)}, u32[]{:S(2)}) copy-start(s32[1,1,3,3]{3,1,2,0:T(1,128)} %param.12) | copy-start | bytes 112
  16.3 19.0 %collective-permute-start.2 = (bf16[2,384,256]{2,1,0:T(8,128)(2,1)S(1)}, bf16[2,384,256]{2,1,0:T(8,128)(2,1)}, u32[]{:S(2)}, u32[]{:S(2)}) collective-permute-start(bf16[2,384,256]{2,1,0:T(8,128)(2,1)S(1)} %get-tuple-element.14), channel_id=1, source_target_pairs={{0,8},{4,12},{8,0},{12,4},{16,24},{20,28},{24,16},{28,20},{1,9},{5... | collective-permute-start | bytes 1179656 | tf_op jit(solution)/shard_map/ppermute | solution.py:20
  18.0 17.4 %collective-permute-start.1 = (bf16[2,384,256]{2,1,0:T(8,128)(2,1)S(1)}, bf16[2,384,256]{2,1,0:T(8,128)(2,1)}, u32[]{:S(2)}, u32[]{:S(2)}) collective-permute-start(bf16[2,384,256]{2,1,0:T(8,128)(2,1)S(1)} %get-tuple-element.13), channel_id=1, source_target_pairs={{0,4},{4,0},{8,12},{12,8},{16,20},{20,16},{24,28},{28,24},{1,5},{5... | collective-permute-start | bytes 1179656 | tf_op jit(solution)/shard_map/ppermute | solution.py:20
  20.2 17.2 %collective-permute-start.4 = (bf16[384,256]{1,0:T(8,128)(2,1)S(1)}, bf16[384,256]{1,0:T(8,128)(2,1)S(1)}, u32[]{:S(2)}, u32[]{:S(2)}) collective-permute-start(bf16[384,256]{1,0:T(8,128)(2,1)S(1)} %convolution_convert_fusion.3), channel_id=1, source_target_pairs={{0,1},{1,2},{2,3},{4,5},{5,6},{6,7},{8,9},{9,10},{10,11},{12,13},{... | collective-permute-start | bytes 589832 | tf_op jit(solution)/shard_map/ppermute | solution.py:16
  39.5 24.0 %collective-permute-start.5 = (bf16[384,256]{1,0:T(8,128)(2,1)S(1)}, bf16[384,256]{1,0:T(8,128)(2,1)S(1)}, u32[]{:S(2)}, u32[]{:S(2)}) collective-permute-start(bf16[384,256]{1,0:T(8,128)(2,1)S(1)} %fusion.15), channel_id=1, source_target_pairs={{1,0},{2,1},{3,2},{5,4},{6,5},{7,6},{9,8},{10,9},{11,10},{13,12},{... | collective-permute-start | bytes 589832 | tf_op jit(solution)/shard_map/ppermute | solution.py:16
  41.0 21.2 %collective-permute-start.8 = (bf16[2,384,256]{2,1,0:T(8,128)(2,1)S(1)}, bf16[2,384,256]{2,1,0:T(8,128)(2,1)S(1)}, u32[]{:S(2)}, u32[]{:S(2)}) collective-permute-start(bf16[2,384,256]{2,1,0:T(8,128)(2,1)S(1)} %get-tuple-element.9), channel_id=1, source_target_pairs={{0,16},{4,20},{8,24},{12,28},{16,0},{20,4},{24,8},{28,12},{1,17},{... | collective-permute-start | bytes 1179656 | tf_op jit(solution)/shard_map/ppermute | solution.py:20
  41.8 20.8 %collective-permute-start.7 = (bf16[2,384,256]{2,1,0:T(8,128)(2,1)S(1)}, bf16[2,384,256]{2,1,0:T(8,128)(2,1)S(1)}, u32[]{:S(2)}, u32[]{:S(2)}) collective-permute-start(bf16[2,384,256]{2,1,0:T(8,128)(2,1)S(1)} %add_bitcast_fusion.4), channel_id=1, source_target_pairs={{0,8},{4,12},{8,0},{12,4},{16,24},{20,28},{24,16},{28,20},{1,9},{5... | collective-permute-start | bytes 1179656 | tf_op jit(solution)/shard_map/ppermute | solution.py:20
  44.4 18.2 %collective-permute-start.6 = (bf16[2,384,256]{2,1,0:T(8,128)(2,1)S(1)}, bf16[2,384,256]{2,1,0:T(8,128)(2,1)S(1)}, u32[]{:S(2)}, u32[]{:S(2)}) collective-permute-start(bf16[2,384,256]{2,1,0:T(8,128)(2,1)S(1)} %get-tuple-element.8), channel_id=1, source_target_pairs={{0,4},{4,0},{8,12},{12,8},{16,20},{20,16},{24,28},{28,24},{1,5},{5... | collective-permute-start | bytes 1179656 | tf_op jit(solution)/shard_map/ppermute | solution.py:20
  45.9 17.6 %collective-permute-start.9 = (bf16[384,256]{1,0:T(8,128)(2,1)S(1)}, bf16[384,256]{1,0:T(8,128)(2,1)S(1)}, u32[]{:S(2)}, u32[]{:S(2)}) collective-permute-start(bf16[384,256]{1,0:T(8,128)(2,1)S(1)} %convolution_convert_fusion.2), channel_id=1, source_target_pairs={{0,1},{1,2},{2,3},{4,5},{5,6},{6,7},{8,9},{9,10},{10,11},{12,13},{... | collective-permute-start | bytes 589832 | tf_op jit(solution)/shard_map/ppermute | solution.py:16
where the time goes:
time: 64.9 us; the launch traced here: 64.6 us
  waiting for transfers between devices  26.1 us (40%)
  starting transfers between devices  19.2 us (30%)
  between operations  6.04 us (9%)
  matrix products  5.84 us (9%)
  local copies, waits for them, and re-layouts  3.93 us (6%)
  other arithmetic  3.43 us (5%)
    ppermute x6, waiting for transfers between devices, from_partner(): lax.ppermute(x, axis, [(i, i ^ 1 << distance) for i in range(lax.axis_siz...  26.1 us
    ppermute x6, starting transfers between devices, from_partner(): lax.ppermute(x, axis, [(i, i ^ 1 << distance) for i in range(lax.axis_siz...  12.1 us
    ppermute x4, starting transfers between devices, from_behind(): return lax.ppermute(block, axis, route)  7.1 us
    unnamed x14, local copies, waits for them, and re-layouts  2.84 us
    dot_general x2, matrix products, operate(): jnp.dot(upper_block, higher_partner, preferred_element_type=jnp.float32)  2.32 us
    another operation x4, other arithmetic, operate(): jnp.stack([select_sum(arrived, chosen[pairing_index]) for pairing_index i...  1.78 us
  transfers between devices with their start and end apart: 10, of which 4 were waited for; matrix products, arithmetic and copies ran while one was open for 16% of the time, Pallas kernels for 0%

commit v1 on v0

v1 whole, which is shorter than its diff:
```python
import functools

import jax
import jax.numpy as jnp
from jax import lax
from jax.experimental import pallas as pl
from jax.experimental.pallas import tpu as pltpu
from jax.sharding import PartitionSpec as P

BLK = 128
LANES = 128

spectrum_center = 1.0
spectrum_halfwidth = 6.0

MESH = pl.DeviceIdType.MESH
F32 = jnp.float32
BF16 = jnp.bfloat16


def mm(a, b):
    return jnp.dot(a, b, preferred_element_type=F32)


def turned(x):
    return x.astype(F32).T


def filter_kernel(
    bits,
    shells,
    vec_hbm,
    local_hbm,
    pair_hbm,
    shell_hbm,
    pair_mask,
    shell_mask,
    matchings,
    out_hbm,
    vec,
    local_raw,
    pair_raw,
    shell_raw,
    own,
    theirs,
    full,
    full_t,
    sym,
    up,
    up_t,
    reply,
    arrived,
    lift,
    from_up,
    from_down,
    acc,
    result,
    load_sem,
    out_sem,
    block_send,
    block_recv,
    edge_send,
    edge_recv,
    down_send,
    down_recv,
    rise_send,
    rise_recv,
):
    halves = vec.shape[1]
    rows = vec.shape[2]
    parts = rows // BLK
    matches = pair_raw.shape[0]
    group = lax.axis_index("grp")
    shell = lax.axis_index("shell")
    has_up = shell < shells - 1
    has_down = shell > 0
    order = list(reversed(range(bits)))

    def digit(b):
        return (group // (1 << b)) % 2

    partner = [group + (1 << b) - 2 * (1 << b) * digit(b) for b in range(bits)]
    role = [(digit(b) + (digit((b + 1) % bits) if bits > 1 else 0) + shell) % 2 for b in range(bits)]
    holds = [role[b] == 1 for b in range(bits)]
    gives = [role[b] == 0 for b in range(bits)]

    columns = lambda h: pl.ds(h * LANES, LANES)
    loads = [pltpu.make_async_copy(pair_hbm, pair_raw, load_sem.at[0])]
    for h in range(halves):
        loads.append(pltpu.make_async_copy(vec_hbm.at[:, columns(h)], vec.at[0, h], load_sem.at[1 + h]))
    loads.append(pltpu.make_async_copy(shell_hbm, shell_raw, load_sem.at[1 + halves]))
    loads.append(pltpu.make_async_copy(local_hbm, local_raw, load_sem.at[2 + halves]))
    for load in loads:
        load.start()

    def block_copy(b):
        return pltpu.make_async_remote_copy(
            src_ref=own.at[b], dst_ref=theirs.at[b], send_sem=block_send.at[b], recv_sem=block_recv.at[b],
            device_id={"grp": partner[b]}, device_id_type=MESH)

    def edge_copy(source, step, b, h):
        return pltpu.make_async_remote_copy(
            src_ref=source, dst_ref=arrived.at[step, b, h], send_sem=edge_send.at[step, b, h],
            recv_sem=edge_recv.at[step, b, h], device_id={"grp": partner[b]}, device_id_type=MESH)

    def given_copy(step, b, h):
        return edge_copy(vec.at[step, h], step, b, h)

    def reply_copy(step, b, h):
        return edge_copy(reply.at[step, b, h], step, b, h)

    def down_copy(step, h):
        return pltpu.make_async_remote_copy(
            src_ref=vec.at[step, h], dst_ref=from_up.at[step, h], send_sem=down_send.at[step, h],
            recv_sem=down_recv.at[step, h], device_id={"shell": shell - 1}, device_id_type=MESH)

    def rise_copy(step, h):
        return pltpu.make_async_remote_copy(
            src_ref=lift.at[step, h], dst_ref=from_down.at[step, h], send_sem=rise_send.at[step, h],
            recv_sem=rise_recv.at[step, h], device_id={"shell": shell + 1}, device_id_type=MESH)

    barrier = pltpu.get_barrier_semaphore()
    for b in range(bits):
        pl.semaphore_signal(barrier, inc=1, device_id={"grp": partner[b]}, device_id_type=MESH)

    @pl.when(has_up)
    def _():
        pl.semaphore_signal(barrier, inc=1, device_id={"shell": shell + 1}, device_id_type=MESH)

    @pl.when(has_down)
    def _():
        pl.semaphore_signal(barrier, inc=1, device_id={"shell": shell - 1}, device_id_type=MESH)

    neighbours = bits + jnp.where(has_up, 1, 0) + jnp.where(has_down, 1, 0)

    flips = [jnp.bitwise_xor(matchings[m, group], group) for m in range(matches)]
    loads[0].wait()
    for at, b in enumerate(order):
        hits = [jnp.where(flips[m] == (1 << b), 1, 0) for m in range(matches)]
        which = jnp.minimum(sum(m * hits[m] for m in range(matches)), matches - 1)
        present = sum(hits)
        for i in range(parts):
            for j in range(parts):
                keep = (pair_mask[which, i, j] * present).astype(F32)
                block = pair_raw[which, pl.ds(i * BLK, BLK), pl.ds(j * BLK, BLK)]
                own[b, pl.ds(i * BLK, BLK), pl.ds(j * BLK, BLK)] = (block.astype(F32) * keep).astype(BF16)
        if at == 0:
            pl.semaphore_wait(barrier, neighbours)

        @pl.when(gives[b])
        def _():
            block_copy(b).start()

    def send_vectors(step, h):
        for b in order:
            @pl.when(gives[b])
            def _():
                given_copy(step, b, h).start()

        @pl.when(has_down)
        def _():
            down_copy(step, h).start()

    def send_lift(step, h):
        @pl.when(has_up)
        def _():
            lift[step, h] = mm(up_t[...], vec[step, h]).astype(BF16)
            rise_copy(step, h).start()

    def send_reply(step, b, h):
        reply[step, b, h] = mm(full_t[b], vec[step, h]).astype(BF16)
        reply_copy(step, b, h).start()

    for h in range(halves):
        loads[1 + h].wait()
        send_vectors(0, h)

    loads[1 + halves].wait()
    for i in range(parts):
        for j in range(parts):
            keep = shell_mask[i, j].astype(F32)
            block = shell_raw[pl.ds(i * BLK, BLK), pl.ds(j * BLK, BLK)].astype(F32) * keep
            up[pl.ds(i * BLK, BLK), pl.ds(j * BLK, BLK)] = block.astype(BF16)
            up_t[pl.ds(j * BLK, BLK), pl.ds(i * BLK, BLK)] = block.T.astype(BF16)
    for h in range(halves):
        send_lift(0, h)

    loads[2 + halves].wait()
    for i in range(parts):
        for j in range(parts):
            here, there = pl.ds(i * BLK, BLK), pl.ds(j * BLK, BLK)
            sym[here, there] = (local_raw[here, there].astype(F32) + turned(local_raw[there, here])).astype(BF16)

    def begin(step, h):
        v = vec[step, h]
        acc[step, h] = mm(sym[...], v) - spectrum_center * v.astype(F32)

    for h in range(halves):
        begin(0, h)

    for b in order:
        @pl.when(holds[b])
        def _():
            block_copy(b).wait_recv()
            for i in range(parts):
                for j in range(parts):
                    here, there = pl.ds(i * BLK, BLK), pl.ds(j * BLK, BLK)
                    k_t = theirs[b, here, there].astype(F32) + turned(own[b, there, here])
                    full_t[b, here, there] = k_t.astype(BF16)
                    full[b, there, here] = k_t.T.astype(BF16)
            for h in range(halves):
                send_reply(0, b, h)

    def gather(step, h):
        @pl.when(has_up)
        def _():
            down_copy(step, h).wait_recv()
            acc[step, h] += mm(up[...], from_up[step, h])

        @pl.when(has_down)
        def _():
            rise_copy(step, h).wait_recv()
            acc[step, h] += from_down[step, h].astype(F32)

        for b in reversed(order):
            @pl.when(holds[b])
            def _():
                given_copy(step, b, h).wait_recv()
                acc[step, h] += mm(full[b], arrived[step, b, h])

        for b in reversed(order):
            @pl.when(gives[b])
            def _():
                reply_copy(step, b, h).wait_recv()
                acc[step, h] += arrived[step, b, h].astype(F32)

    for h in range(halves):
        gather(0, h)
        vec[1, h] = (acc[0, h] * (1.0 / spectrum_halfwidth)).astype(BF16)
        send_vectors(1, h)
        for b in order:
            @pl.when(holds[b])
            def _():
                send_reply(1, b, h)
        send_lift(1, h)
        begin(1, h)

    stores = []
    for h in range(halves):
        gather(1, h)
        result[h] = (acc[1, h] * (2.0 / spectrum_halfwidth) - vec[0, h].astype(F32)).astype(BF16)
        store = pltpu.make_async_copy(result.at[h], out_hbm.at[:, columns(h)], out_sem.at[h])
        store.start()
        stores.append(store)

    for b in range(bits):
        @pl.when(gives[b])
        def _():
            block_copy(b).wait_send()
            for step in range(2):
                for h in range(halves):
                    given_copy(step, b, h).wait_send()

        @pl.when(holds[b])
        def _():
            for step in range(2):
                for h in range(halves):
                    reply_copy(step, b, h).wait_send()

    @pl.when(has_down)
    def _():
        for step in range(2):
            for h in range(halves):
                down_copy(step, h).wait_send()

    @pl.when(has_up)
    def _():
        for step in range(2):
            for h in range(halves):
                rise_copy(step, h).wait_send()

    for store in stores:
        store.wait()


def on_device(bits, shells, vectors, local_block, pair_blocks, pair_masks, shell_block, shell_mask, matchings):
    rows, width = vectors.shape[2:]
    matches = pair_blocks.shape[2]
    halves = width // LANES
    square = (rows, rows)
    tall = (halves, rows, LANES)
    out = pl.pallas_call(
        functools.partial(filter_kernel, bits, shells),
        out_shape=jax.ShapeDtypeStruct((rows, width), BF16),
        in_specs=[pl.BlockSpec(memory_space=pl.ANY)] * 4 + [pl.BlockSpec(memory_space=pltpu.SMEM)] * 3,
        out_specs=pl.BlockSpec(memory_space=pl.ANY),
        scratch_shapes=[
            pltpu.VMEM((2,) + tall, BF16),
            pltpu.VMEM(square, BF16),
            pltpu.VMEM((matches,) + square, BF16),
            pltpu.VMEM(square, BF16),
            pltpu.VMEM((bits,) + square, BF16),
            pltpu.VMEM((bits,) + square, BF16),
            pltpu.VMEM((bits,) + square, BF16),
            pltpu.VMEM((bits,) + square, BF16),
            pltpu.VMEM(square, BF16),
            pltpu.VMEM(square, BF16),
            pltpu.VMEM(square, BF16),
            pltpu.VMEM((2, bits) + tall, BF16),
            pltpu.VMEM((2, bits) + tall, BF16),
            pltpu.VMEM((2,) + tall, BF16),
            pltpu.VMEM((2,) + tall, BF16),
            pltpu.VMEM((2,) + tall, BF16),
            pltpu.VMEM((2,) + tall, F32),
            pltpu.VMEM(tall, BF16),
            pltpu.SemaphoreType.DMA((3 + halves,)),
            pltpu.SemaphoreType.DMA((halves,)),
            pltpu.SemaphoreType.DMA((bits,)),
            pltpu.SemaphoreType.DMA((bits,)),
            pltpu.SemaphoreType.DMA((2, bits, halves)),
            pltpu.SemaphoreType.DMA((2, bits, halves)),
            pltpu.SemaphoreType.DMA((2, halves)),
            pltpu.SemaphoreType.DMA((2, halves)),
            pltpu.SemaphoreType.DMA((2, halves)),
            pltpu.SemaphoreType.DMA((2, halves)),
        ],
        compiler_params=pltpu.CompilerParams(
            collective_id=0, has_side_effects=True, vmem_limit_bytes=40 * 1024 * 1024
        ),
    )(
        vectors[0, 0],
        local_block[0, 0],
        pair_blocks[0, 0],
        shell_block[0, 0],
        pair_masks[0, 0],
        shell_mask[0, 0],
        matchings,
    )
    return out[None, None]


def solution(mesh):
    sizes = dict(mesh.shape)
    bits = sizes["grp"].bit_length() - 1
    in_specs = (
        P("grp", "shell", None, None),
        P("grp", "shell", None, None),
        P("grp", "shell", None, None, None),
        P("grp", "shell", None, None, None),
        P("grp", "shell", None, None),
        P("grp", "shell", None, None),
        P(),
    )
    out_specs = P("grp", "shell", None, None)
    return jax.shard_map(
        functools.partial(on_device, bits, sizes["shell"]),
        mesh=mesh, in_specs=in_specs, out_specs=out_specs, check_vma=False,
    )
```

time: 64.9 us -> 38.4 us (0.59)
  Pallas kernels: 0 us -> 32 us
  waiting for transfers between devices: 26.1 us -> 0 us
  starting transfers between devices: 19.2 us -> 0 us
  between operations: 6.04 us -> 0.02 us
  matrix products: 5.84 us -> 0 us
  other arithmetic: 3.43 us -> 0 us
  local copies, waits for them, and re-layouts: 3.93 us -> 6.08 us
    pallas_call x0 -> x1, Pallas kernels: none -> 32 us  [on_device(): pl.pallas_call(functools.partial(filter_kernel, bits, shells), out_shape=...]
    ppermute x10 -> x0, waiting for transfers between devices: 26.1 us -> none  [the longest x6 26.1 us: from_partner(): lax.ppermute(x, axis, [(i, i ^ 1 << distance) for i in range(lax.axis_siz...]
    ppermute x10 -> x0, starting transfers between devices: 19.2 us -> none  [the longest x6 12.1 us: from_partner(): lax.ppermute(x, axis, [(i, i ^ 1 << distance) for i in range(lax.axis_siz...]
    dot_general x12 -> x0, matrix products: 5.84 us -> none  [the longest x2 2.32 us: operate(): jnp.dot(upper_block, higher_partner, preferred_element_type=jnp.float32)]
    unnamed x14 -> x17, local copies, waits for them, and re-layouts: 2.84 us -> 6.08 us
    another operation x4 -> x0, other arithmetic: 1.78 us -> none  [operate(): jnp.stack([select_sum(arrived, chosen[pairing_index]) for pairing_index i...]
    xor x1 -> x0, other arithmetic: 0.76 us -> none  [on_device(): flip_bits = jnp.bitwise_xor(matchings[:, group_index], group_index)]
  transfers between devices with their start and end apart: 10 -> 0, of which waited for: 4 -> 0; matrix products, arithmetic and copies ran while one was open for 16% -> 0% of each run, Pallas kernels for 0% -> 0%
where the time goes in v1:
time: 38.4 us; the launch traced here: 38.1 us
  Pallas kernels  32 us (83%)
  local copies, waits for them, and re-layouts  6.08 us (16%)
    pallas_call x1, Pallas kernels, on_device(): pl.pallas_call(functools.partial(filter_kernel, bits, shells), out_shape=...  32 us
    unnamed x17, local copies, waits for them, and re-layouts  6.08 us

profile of v1, /device:TPU:0, one launch (start us, length us, event | category | flops | bytes accessed | tf_op | source)
XLA Modules:
  0.0 38.1 jit_solution(15656186261775123475)
XLA Ops:
  0.0 0.0 copy-start.6
  0.0 0.0 copy-start.5
  0.0 0.7 %copy-done.6 = s32[1,1,3,3]{3,1,2,0:T(1,128)S(1)} copy-done((s32[1,1,3,3]{3,1,2,0:T(1,128)S(1)}, s32[1,1,3,3]{3,1,2,0:T(1,128)}, u32[]{:S(2)}) %copy-start.6) | copy-done | bytes 60
  0.7 0.0 copy-done.5
  0.7 0.0 copy-start.4
  0.7 0.7 %copy-done.4 = s32[3,8]{1,0:T(4,128)S(1)} copy-done((s32[3,8]{1,0:T(4,128)S(1)}, s32[3,8]{1,0:T(4,128)}, u32[]{:S(2)}) %copy-start.4) | copy-done | bytes 120
  1.4 0.0 copy-start
  1.4 1.2 %copy-done = bf16[1,1,3,384,384]{4,3,2,1,0:T(8,128)(2,1)S(1)} copy-done((bf16[1,1,3,384,384]{4,3,2,1,0:T(8,128)(2,1)S(1)}, bf16[1,1,3,384,384]{4,3,2,1,0:T(8,128)(2,1)}, u32[]{:S(2)}) %copy-start) | copy-done | bytes 884760
  2.6 0.0 copy-start.1
  2.6 1.0 %copy-done.1 = bf16[1,1,384,384]{3,2,1,0:T(8,128)(2,1)S(1)} copy-done((bf16[1,1,384,384]{3,2,1,0:T(8,128)(2,1)S(1)}, bf16[1,1,384,384]{3,2,1,0:T(8,128)(2,1)}, u32[]{:S(2)}) %copy-start.1) | copy-done | bytes 294936
  3.5 0.0 copy-start.2
  3.5 1.0 %copy-done.2 = bf16[1,1,384,384]{3,2,1,0:T(8,128)(2,1)S(1)} copy-done((bf16[1,1,384,384]{3,2,1,0:T(8,128)(2,1)S(1)}, bf16[1,1,384,384]{3,2,1,0:T(8,128)(2,1)}, u32[]{:S(2)}) %copy-start.2) | copy-done | bytes 294936
  4.5 0.0 copy-start.3
  4.5 0.9 %copy-done.3 = bf16[1,1,384,256]{3,2,1,0:T(8,128)(2,1)S(1)} copy-done((bf16[1,1,384,256]{3,2,1,0:T(8,128)(2,1)S(1)}, bf16[1,1,384,256]{3,2,1,0:T(8,128)(2,1)}, u32[]{:S(2)}) %copy-start.3) | copy-done | bytes 196632
  5.4 32.0 %shard_map.73 = bf16[384,256]{1,0:T(8,128)(2,1)S(1)} custom-call(bf16[384,256]{1,0:T(8,128)(2,1)S(1)} %bitcast.15, bf16[384,384]{1,0:T(8,128)(2,1)S(1)} %bitcast.13, bf16[3,384,384]{2,1,0:T(8,128)(2,1)S(1)} %bitcast.11, bf16[384,384]{1,0:T(8,128)(2,1)S(1)} %bitcast.14, s32[3,3,3]{2,1,0:T(4,128)S(1)} %bitcast.16, s32[3,3]{1,0:T(4,128)S(1)} %bitcast.17, ...), custom_call_target="tpu_custom_call" | custom-call | tf_op jit(solution)/shard_map/pallas_call | solution.py:292
  37.4 0.7 %copy.15 = bf16[1,1,384,256]{3,2,1,0:T(8,128)(2,1)} copy(bf16[1,1,384,256]{3,2,1,0:T(8,128)(2,1)S(1)} %bitcast.12) | data formatting | bytes 393216
  (2 shorter events, 0.0 us)
Async XLA Ops:
  0.0 0.7 %copy-start.6 = (s32[1,1,3,3]{3,1,2,0:T(1,128)S(1)}, s32[1,1,3,3]{3,1,2,0:T(1,128)}, u32[]{:S(2)}) copy-start(s32[1,1,3,3]{3,1,2,0:T(1,128)} %param.12) | copy-start | bytes 112
  0.0 0.7 %copy-start.5 = (s32[1,1,3,3,3]{4,1,3,2,0:T(1,128)S(1)}, s32[1,1,3,3,3]{4,1,3,2,0:T(1,128)}, u32[]{:S(2)}) copy-start(s32[1,1,3,3,3]{4,1,3,2,0:T(1,128)} %param.10) | copy-start | bytes 328
  0.7 0.7 %copy-start.4 = (s32[3,8]{1,0:T(4,128)S(1)}, s32[3,8]{1,0:T(4,128)}, u32[]{:S(2)}) copy-start(s32[3,8]{1,0:T(4,128)} %matchings.1) | copy-start | bytes 292
  1.4 1.2 %copy-start = (bf16[1,1,3,384,384]{4,3,2,1,0:T(8,128)(2,1)S(1)}, bf16[1,1,3,384,384]{4,3,2,1,0:T(8,128)(2,1)}, u32[]{:S(2)}) copy-start(bf16[1,1,3,384,384]{4,3,2,1,0:T(8,128)(2,1)} %param.9) | copy-start | bytes 2654212
  2.6 1.0 %copy-start.1 = (bf16[1,1,384,384]{3,2,1,0:T(8,128)(2,1)S(1)}, bf16[1,1,384,384]{3,2,1,0:T(8,128)(2,1)}, u32[]{:S(2)}) copy-start(bf16[1,1,384,384]{3,2,1,0:T(8,128)(2,1)} %param.8) | copy-start | bytes 884740
  3.5 1.0 %copy-start.2 = (bf16[1,1,384,384]{3,2,1,0:T(8,128)(2,1)S(1)}, bf16[1,1,384,384]{3,2,1,0:T(8,128)(2,1)}, u32[]{:S(2)}) copy-start(bf16[1,1,384,384]{3,2,1,0:T(8,128)(2,1)} %param.11) | copy-start | bytes 884740
  4.5 0.9 %copy-start.3 = (bf16[1,1,384,256]{3,2,1,0:T(8,128)(2,1)S(1)}, bf16[1,1,384,256]{3,2,1,0:T(8,128)(2,1)}, u32[]{:S(2)}) copy-start(bf16[1,1,384,256]{3,2,1,0:T(8,128)(2,1)} %param.7) | copy-start | bytes 589828

commit v2 on v1

--- a/solution.py
+++ b/solution.py
@@ -33,10 +33,13 @@
     local_hbm,
     pair_hbm,
     shell_hbm,
+    pair_mask_hbm,
+    shell_mask_hbm,
+    matchings_hbm,
+    out,
     pair_mask,
     shell_mask,
     matchings,
-    out_hbm,
     vec,
     local_raw,
     pair_raw,
@@ -54,9 +57,7 @@
     from_up,
     from_down,
     acc,
-    result,
     load_sem,
-    out_sem,
     block_send,
     block_recv,
     edge_send,
@@ -90,7 +91,12 @@
         loads.append(pltpu.make_async_copy(vec_hbm.at[:, columns(h)], vec.at[0, h], load_sem.at[1 + h]))
     loads.append(pltpu.make_async_copy(shell_hbm, shell_raw, load_sem.at[1 + halves]))
     loads.append(pltpu.make_async_copy(local_hbm, local_raw, load_sem.at[2 + halves]))
-    for load in loads:
+    tables = [
+        pltpu.make_async_copy(matchings_hbm, matchings, load_sem.at[3 + halves]),
+        pltpu.make_async_copy(pair_mask_hbm, pair_mask, load_sem.at[4 + halves]),
+        pltpu.make_async_copy(shell_mask_hbm, shell_mask, load_sem.at[5 + halves]),
+    ]
+    for load in tables + loads:
         load.start()
 
     def block_copy(b):
@@ -133,6 +139,8 @@
 
     neighbours = bits + jnp.where(has_up, 1, 0) + jnp.where(has_down, 1, 0)
 
+    for table in tables:
+        table.wait()
     flips = [jnp.bitwise_xor(matchings[m, group], group) for m in range(matches)]
     loads[0].wait()
     for at, b in enumerate(order):
@@ -141,7 +149,7 @@
         present = sum(hits)
         for i in range(parts):
             for j in range(parts):
-                keep = (pair_mask[which, i, j] * present).astype(F32)
+                keep = (pair_mask[which * parts + i, 0, j] * present).astype(F32)
                 block = pair_raw[which, pl.ds(i * BLK, BLK), pl.ds(j * BLK, BLK)]
                 own[b, pl.ds(i * BLK, BLK), pl.ds(j * BLK, BLK)] = (block.astype(F32) * keep).astype(BF16)
         if at == 0:
@@ -178,7 +186,7 @@
     loads[1 + halves].wait()
     for i in range(parts):
         for j in range(parts):
-            keep = shell_mask[i, j].astype(F32)
+            keep = shell_mask[i, 0, j].astype(F32)
             block = shell_raw[pl.ds(i * BLK, BLK), pl.ds(j * BLK, BLK)].astype(F32) * keep
             up[pl.ds(i * BLK, BLK), pl.ds(j * BLK, BLK)] = block.astype(BF16)
             up_t[pl.ds(j * BLK, BLK), pl.ds(i * BLK, BLK)] = block.T.astype(BF16)
@@ -198,18 +206,43 @@
     for h in range(halves):
         begin(0, h)
 
-    for b in order:
+    def each_block(work):
+        for i in range(parts):
+            for j in range(parts):
+                work(pl.ds(i * BLK, BLK), pl.ds(j * BLK, BLK))
+
+    for b in range(bits):
         @pl.when(holds[b])
         def _():
+            def turn(here, there):
+                full_t[b, here, there] = turned(own[b, there, here]).astype(BF16)
+
+            each_block(turn)
+
+    for b in range(bits):
+        @pl.when(holds[b])
+        def _():
+            def join(here, there):
+                k_t = theirs[b, here, there].astype(F32) + full_t[b, here, there].astype(F32)
+                full_t[b, here, there] = k_t.astype(BF16)
+
             block_copy(b).wait_recv()
-            for i in range(parts):
-                for j in range(parts):
-                    here, there = pl.ds(i * BLK, BLK), pl.ds(j * BLK, BLK)
-                    k_t = theirs[b, here, there].astype(F32) + turned(own[b, there, here])
-                    full_t[b, here, there] = k_t.astype(BF16)
-                    full[b, there, here] = k_t.T.astype(BF16)
-            for h in range(halves):
+            each_block(join)
+            send_reply(0, b, 0)
+
+    for h in range(1, halves):
+        for b in order:
+            @pl.when(holds[b])
+            def _():
                 send_reply(0, b, h)
+
+    for b in range(bits):
+        @pl.when(holds[b])
+        def _():
+            def turn_back(here, there):
+                full[b, there, here] = turned(full_t[b, here, there]).astype(BF16)
+
+            each_block(turn_back)
 
     def gather(step, h):
         @pl.when(has_up)
@@ -245,13 +278,10 @@
         send_lift(1, h)
         begin(1, h)
 
-    stores = []
     for h in range(halves):
         gather(1, h)
-        result[h] = (acc[1, h] * (2.0 / spectrum_halfwidth) - vec[0, h].astype(F32)).astype(BF16)
-        store = pltpu.make_async_copy(result.at[h], out_hbm.at[:, columns(h)], out_sem.at[h])
-        store.start()
-        stores.append(store)
+        y2 = acc[1, h] * (2.0 / spectrum_halfwidth) - vec[0, h].astype(F32)
+        out[:, columns(h)] = y2.astype(BF16)
 
     for b in range(bits):
         @pl.when(gives[b])
@@ -279,22 +309,25 @@
             for h in range(halves):
                 rise_copy(step, h).wait_send()
 
-    for store in stores:
-        store.wait()
-
 
 def on_device(bits, shells, vectors, local_block, pair_blocks, pair_masks, shell_block, shell_mask, matchings):
     rows, width = vectors.shape[2:]
     matches = pair_blocks.shape[2]
     halves = width // LANES
+    parts = pair_masks.shape[-1]
+    pair_masks = pair_masks.reshape(matches * parts, 1, parts)
+    shell_mask = shell_mask.reshape(parts, 1, parts)
     square = (rows, rows)
     tall = (halves, rows, LANES)
     out = pl.pallas_call(
         functools.partial(filter_kernel, bits, shells),
         out_shape=jax.ShapeDtypeStruct((rows, width), BF16),
-        in_specs=[pl.BlockSpec(memory_space=pl.ANY)] * 4 + [pl.BlockSpec(memory_space=pltpu.SMEM)] * 3,
-        out_specs=pl.BlockSpec(memory_space=pl.ANY),
+        in_specs=[pl.BlockSpec(memory_space=pltpu.HBM)] * 7,
+        out_specs=pl.BlockSpec(memory_space=pltpu.VMEM),
         scratch_shapes=[
+            pltpu.SMEM(pair_masks.shape, jnp.int32),
+            pltpu.SMEM(shell_mask.shape, jnp.int32),
+            pltpu.SMEM(matchings.shape, jnp.int32),
             pltpu.VMEM((2,) + tall, BF16),
             pltpu.VMEM(square, BF16),
             pltpu.VMEM((matches,) + square, BF16),
@@ -312,9 +345,7 @@
             pltpu.VMEM((2,) + tall, BF16),
             pltpu.VMEM((2,) + tall, BF16),
             pltpu.VMEM((2,) + tall, F32),
-            pltpu.VMEM(tall, BF16),
-            pltpu.SemaphoreType.DMA((3 + halves,)),
-            pltpu.SemaphoreType.DMA((halves,)),
+            pltpu.SemaphoreType.DMA((6 + halves,)),
             pltpu.SemaphoreType.DMA((bits,)),
             pltpu.SemaphoreType.DMA((bits,)),
             pltpu.SemaphoreType.DMA((2, bits, halves)),
@@ -325,15 +356,15 @@
             pltpu.SemaphoreType.DMA((2, halves)),
         ],
         compiler_params=pltpu.CompilerParams(
-            collective_id=0, has_side_effects=True, vmem_limit_bytes=40 * 1024 * 1024
+            collective_id=0, has_side_effects=True, vmem_limit_bytes=int(63.5 * 1024 * 1024)
         ),
     )(
         vectors[0, 0],
         local_block[0, 0],
         pair_blocks[0, 0],
         shell_block[0, 0],
-        pair_masks[0, 0],
-        shell_mask[0, 0],
+        pair_masks,
+        shell_mask,
         matchings,
     )
     return out[None, None]

time: 38.4 us -> 32.3 us (0.84)
  local copies, waits for them, and re-layouts: 6.08 us -> 1.62 us
  Pallas kernels: 32 us -> 30.4 us
    unnamed x17 -> x1, local copies, waits for them, and re-layouts: 6.08 us -> 1.62 us
    pallas_call x1, Pallas kernels: 32 us -> 30.4 us  [on_device(): pl.pallas_call(functools.partial(filter_kernel, bits, shells), out_shape=...]
where the time goes in v2:
time: 32.3 us; the launch traced here: 32 us
  Pallas kernels  30.4 us (94%)
  local copies, waits for them, and re-layouts  1.62 us (5%)
    pallas_call x1, Pallas kernels, on_device(): pl.pallas_call(functools.partial(filter_kernel, bits, shells), out_shape=...  30.4 us
    unnamed x1, local copies, waits for them, and re-layouts  1.62 us

profile of v2, /device:TPU:0, one launch (start us, length us, event | category | flops | bytes accessed | tf_op | source)
XLA Modules:
  0.0 32.0 jit_solution(9526425657285634158)
XLA Ops:
  0.0 30.4 %shard_map.73 = bf16[384,256]{1,0:T(8,128)(2,1)} custom-call(bf16[384,256]{1,0:T(8,128)(2,1)} %bitcast.11, bf16[384,384]{1,0:T(8,128)(2,1)} %bitcast.9, bf16[3,384,384]{2,1,0:T(8,128)(2,1)} %bitcast.7, bf16[384,384]{1,0:T(8,128)(2,1)} %bitcast.10, s32[9,1,3]{2,1,0:T(1,128)} %bitcast.12, s32[3,1,3]{2,1,0:T(1,128)} %bitcast.13, s32[3,8]{1,0:T(4,128)} %matchings_hbm.1), custom_call_target="tpu_custom_call" | custom-call | tf_op jit(solution)/shard_map/pallas_call | solution.py:322
  30.4 1.6 %copy.15 = bf16[1,1,384,256]{3,2,1,0:T(8,128)(2,1)} copy(bf16[1,1,384,256]{3,2,1,0:T(8,128)(2,1)} %bitcast.8) | data formatting | bytes 393216

commit v3 on v2

--- a/solution.py
+++ b/solution.py
@@ -356,17 +356,20 @@
             pltpu.SemaphoreType.DMA((2, halves)),
         ],
         compiler_params=pltpu.CompilerParams(
-            collective_id=0, has_side_effects=True, vmem_limit_bytes=int(63.5 * 1024 * 1024)
+            collective_id=0, has_side_effects=True, vmem_limit_bytes=40 * 1024 * 1024
         ),
-    )(
-        vectors[0, 0],
-        local_block[0, 0],
-        pair_blocks[0, 0],
-        shell_block[0, 0],
-        pair_masks,
-        shell_mask,
-        matchings,
-    )
+    )(*[
+        pltpu.with_memory_space_constraint(x, pltpu.HBM)
+        for x in (
+            vectors[0, 0],
+            local_block[0, 0],
+            pair_blocks[0, 0],
+            shell_block[0, 0],
+            pair_masks,
+            shell_mask,
+            matchings,
+        )
+    ])
     return out[None, None]
 
 

time: 32.3 us -> 30.6 us (0.947)
  local copies, waits for them, and re-layouts: 1.62 us -> 0.68 us
  Pallas kernels: 30.4 us -> 29.7 us
    unnamed x1, local copies, waits for them, and re-layouts: 1.62 us -> 0.68 us
    pallas_call x1, Pallas kernels: 30.4 us -> 29.7 us  [on_device(): pl.pallas_call(functools.partial(filter_kernel, bits, shells), out_shape=...]
where the time goes in v3:
time: 30.6 us; the launch traced here: 30.4 us
  Pallas kernels  29.7 us (97%)
  local copies, waits for them, and re-layouts  0.68 us (2%)
    pallas_call x1, Pallas kernels, on_device(): pl.pallas_call(functools.partial(filter_kernel, bits, shells), out_shape=...  29.7 us
    unnamed x1, local copies, waits for them, and re-layouts  0.68 us

profile of v3, /device:TPU:0, one launch (start us, length us, event | category | flops | bytes accessed | tf_op | source)
XLA Modules:
  0.0 30.4 jit_solution(10590743003520020693)
XLA Ops:
  0.0 29.7 %shard_map.73 = bf16[384,256]{1,0:T(8,128)(2,1)S(1)} custom-call(bf16[384,256]{1,0:T(8,128)(2,1)} %bitcast.11, bf16[384,384]{1,0:T(8,128)(2,1)} %bitcast.9, bf16[3,384,384]{2,1,0:T(8,128)(2,1)} %bitcast.8, bf16[384,384]{1,0:T(8,128)(2,1)} %bitcast.10, s32[9,1,3]{2,1,0:T(1,128)} %bitcast.12, s32[3,1,3]{2,1,0:T(1,128)} %bitcast.13, s32[3,8]{1,0:T(4,128)} %matchings_hbm.1), custom_call_target="tpu_custom_call" | custom-call | tf_op jit(solution)/shard_map/pallas_call | solution.py:322
  29.7 0.7 %copy.15 = bf16[1,1,384,256]{3,2,1,0:T(8,128)(2,1)} copy(bf16[1,1,384,256]{3,2,1,0:T(8,128)(2,1)S(1)} %bitcast.7) | data formatting | bytes 393216

commit v4 on v3

--- a/solution.py
+++ b/solution.py
@@ -20,10 +20,6 @@
 
 def mm(a, b):
     return jnp.dot(a, b, preferred_element_type=F32)
-
-
-def turned(x):
-    return x.astype(F32).T
 
 
 def filter_kernel(
@@ -139,57 +135,63 @@
 
     neighbours = bits + jnp.where(has_up, 1, 0) + jnp.where(has_down, 1, 0)
 
+    def send_down(step, h):
+        @pl.when(has_down)
+        def _():
+            down_copy(step, h).start()
+
+    def send_vectors(step, h):
+        for b in order:
+            @pl.when(gives[b])
+            def _():
+                given_copy(step, b, h).start()
+
+        send_down(step, h)
+
+    def send_lift(step, h):
+        @pl.when(has_up)
+        def _():
+            lift[step, h] = mm(up_t[...], vec[step, h]).astype(BF16)
+            rise_copy(step, h).start()
+
+    def send_reply(step, b, h):
+        reply[step, b, h] = mm(full_t[b], vec[step, h]).astype(BF16)
+        reply_copy(step, b, h).start()
+
+    loads[1].wait()
+    pl.semaphore_wait(barrier, neighbours)
+    send_vectors(0, 0)
+
     for table in tables:
         table.wait()
     flips = [jnp.bitwise_xor(matchings[m, group], group) for m in range(matches)]
     loads[0].wait()
-    for at, b in enumerate(order):
+    for b in order:
         hits = [jnp.where(flips[m] == (1 << b), 1, 0) for m in range(matches)]
         which = jnp.minimum(sum(m * hits[m] for m in range(matches)), matches - 1)
         present = sum(hits)
         for i in range(parts):
             for j in range(parts):
                 keep = (pair_mask[which * parts + i, 0, j] * present).astype(F32)
+                keep = jnp.broadcast_to(keep, (BLK, BLK)).astype(BF16)
                 block = pair_raw[which, pl.ds(i * BLK, BLK), pl.ds(j * BLK, BLK)]
-                own[b, pl.ds(i * BLK, BLK), pl.ds(j * BLK, BLK)] = (block.astype(F32) * keep).astype(BF16)
-        if at == 0:
-            pl.semaphore_wait(barrier, neighbours)
+                own[b, pl.ds(i * BLK, BLK), pl.ds(j * BLK, BLK)] = block * keep
 
         @pl.when(gives[b])
         def _():
             block_copy(b).start()
 
-    def send_vectors(step, h):
-        for b in order:
-            @pl.when(gives[b])
-            def _():
-                given_copy(step, b, h).start()
-
-        @pl.when(has_down)
-        def _():
-            down_copy(step, h).start()
-
-    def send_lift(step, h):
-        @pl.when(has_up)
-        def _():
-            lift[step, h] = mm(up_t[...], vec[step, h]).astype(BF16)
-            rise_copy(step, h).start()
-
-    def send_reply(step, b, h):
-        reply[step, b, h] = mm(full_t[b], vec[step, h]).astype(BF16)
-        reply_copy(step, b, h).start()
-
-    for h in range(halves):
+    for h in range(1, halves):
         loads[1 + h].wait()
-        send_vectors(0, h)
+        send_down(0, h)
 
     loads[1 + halves].wait()
     for i in range(parts):
         for j in range(parts):
-            keep = shell_mask[i, 0, j].astype(F32)
-            block = shell_raw[pl.ds(i * BLK, BLK), pl.ds(j * BLK, BLK)].astype(F32) * keep
-            up[pl.ds(i * BLK, BLK), pl.ds(j * BLK, BLK)] = block.astype(BF16)
-            up_t[pl.ds(j * BLK, BLK), pl.ds(i * BLK, BLK)] = block.T.astype(BF16)
+            keep = jnp.broadcast_to(shell_mask[i, 0, j].astype(F32), (BLK, BLK)).astype(BF16)
+            block = shell_raw[pl.ds(i * BLK, BLK), pl.ds(j * BLK, BLK)] * keep
+            up[pl.ds(i * BLK, BLK), pl.ds(j * BLK, BLK)] = block
+            up_t[pl.ds(j * BLK, BLK), pl.ds(i * BLK, BLK)] = block.T
     for h in range(halves):
         send_lift(0, h)
 
@@ -197,7 +199,7 @@
     for i in range(parts):
         for j in range(parts):
             here, there = pl.ds(i * BLK, BLK), pl.ds(j * BLK, BLK)
-            sym[here, there] = (local_raw[here, there].astype(F32) + turned(local_raw[there, here])).astype(BF16)
+            sym[here, there] = (local_raw[here, there].astype(F32) + local_raw[there, here].T.astype(F32)).astype(BF16)
 
     def begin(step, h):
         v = vec[step, h]
@@ -215,7 +217,7 @@
         @pl.when(holds[b])
         def _():
             def turn(here, there):
-                full_t[b, here, there] = turned(own[b, there, here]).astype(BF16)
+                full_t[b, here, there] = own[b, there, here].T
 
             each_block(turn)
 
@@ -229,6 +231,14 @@
             block_copy(b).wait_recv()
             each_block(join)
             send_reply(0, b, 0)
+
+        if b == 0:
+            for c in order:
+                @pl.when(gives[c])
+                def _():
+                    block_copy(c).wait_send()
+                    for h in range(1, halves):
+                        given_copy(0, c, h).start()
 
     for h in range(1, halves):
         for b in order:
@@ -240,7 +250,7 @@
         @pl.when(holds[b])
         def _():
             def turn_back(here, there):
-                full[b, there, here] = turned(full_t[b, here, there]).astype(BF16)
+                full[b, there, here] = full_t[b, here, there].T
 
             each_block(turn_back)
 
@@ -286,7 +296,6 @@
     for b in range(bits):
         @pl.when(gives[b])
         def _():
-            block_copy(b).wait_send()
             for step in range(2):
                 for h in range(halves):
                     given_copy(step, b, h).wait_send()

time: 30.6 us -> 32.7 us (1.069)
  Pallas kernels: 29.7 us -> 31.9 us
    pallas_call x1, Pallas kernels: 29.7 us -> 31.9 us  [on_device(): pl.pallas_call(functools.partial(filter_kernel, bits, shells), out_shape=...]
where the time goes in v4:
time: 32.7 us; the launch traced here: 32.6 us
  Pallas kernels  31.9 us (98%)
  local copies, waits for them, and re-layouts  0.68 us (2%)
    pallas_call x1, Pallas kernels, on_device(): pl.pallas_call(functools.partial(filter_kernel, bits, shells), out_shape=...  31.9 us
    unnamed x1, local copies, waits for them, and re-layouts  0.68 us

profile of v4, /device:TPU:0, one launch (start us, length us, event | category | flops | bytes accessed | tf_op | source)
XLA Modules:
  0.0 32.6 jit_solution(6105705163476829876)
XLA Ops:
  0.0 31.9 %shard_map.73 = bf16[384,256]{1,0:T(8,128)(2,1)S(1)} custom-call(bf16[384,256]{1,0:T(8,128)(2,1)} %bitcast.11, bf16[384,384]{1,0:T(8,128)(2,1)} %bitcast.9, bf16[3,384,384]{2,1,0:T(8,128)(2,1)} %bitcast.8, bf16[384,384]{1,0:T(8,128)(2,1)} %bitcast.10, s32[9,1,3]{2,1,0:T(1,128)} %bitcast.12, s32[3,1,3]{2,1,0:T(1,128)} %bitcast.13, s32[3,8]{1,0:T(4,128)} %matchings_hbm.1), custom_call_target="tpu_custom_call" | custom-call | tf_op jit(solution)/shard_map/pallas_call | solution.py:331
  31.9 0.7 %copy.15 = bf16[1,1,384,256]{3,2,1,0:T(8,128)(2,1)} copy(bf16[1,1,384,256]{3,2,1,0:T(8,128)(2,1)S(1)} %bitcast.7) | data formatting | bytes 393216

commit v5 on v4

--- a/solution.py
+++ b/solution.py
@@ -183,7 +183,7 @@
 
     for h in range(1, halves):
         loads[1 + h].wait()
-        send_down(0, h)
+        send_vectors(0, h)
 
     loads[1 + halves].wait()
     for i in range(parts):
@@ -232,14 +232,6 @@
             each_block(join)
             send_reply(0, b, 0)
 
-        if b == 0:
-            for c in order:
-                @pl.when(gives[c])
-                def _():
-                    block_copy(c).wait_send()
-                    for h in range(1, halves):
-                        given_copy(0, c, h).start()
-
     for h in range(1, halves):
         for b in order:
             @pl.when(holds[b])
@@ -296,6 +288,7 @@
     for b in range(bits):
         @pl.when(gives[b])
         def _():
+            block_copy(b).wait_send()
             for step in range(2):
                 for h in range(halves):
                     given_copy(step, b, h).wait_send()

time: 32.7 us -> 34 us (1.040)
  the two profiles are of different devices: /device:TPU:0 before, /device:TPU:1 now
where the time goes in v5:
time: 34 us; the launch traced here: 33.8 us
  Pallas kernels  33.2 us (98%)
  local copies, waits for them, and re-layouts  0.68 us (2%)
    pallas_call x1, Pallas kernels, on_device(): pl.pallas_call(functools.partial(filter_kernel, bits, shells), out_shape=...  33.2 us

profile of v5, /device:TPU:1, one launch (start us, length us, event | category | flops | bytes accessed | tf_op | source)
XLA Modules:
  0.0 33.8 jit_solution(13234802488694275722)
XLA Ops:
  0.0 33.2 %shard_map.73 = bf16[384,256]{1,0:T(8,128)(2,1)S(1)} custom-call(bf16[384,256]{1,0:T(8,128)(2,1)} %bitcast.11, bf16[384,384]{1,0:T(8,128)(2,1)} %bitcast.9, bf16[3,384,384]{2,1,0:T(8,128)(2,1)} %bitcast.8, bf16[384,384]{1,0:T(8,128)(2,1)} %bitcast.10, s32[9,1,3]{2,1,0:T(1,128)} %bitcast.12, s32[3,1,3]{2,1,0:T(1,128)} %bitcast.13, s32[3,8]{1,0:T(4,128)} %matchings_hbm.1), custom_call_target="tpu_custom_call" | custom-call | tf_op jit(solution)/shard_map/pallas_call | solution.py:324
  33.2 0.7 %copy.15 = bf16[1,1,384,256]{3,2,1,0:T(8,128)(2,1)} copy(bf16[1,1,384,256]{3,2,1,0:T(8,128)(2,1)S(1)} %bitcast.7) | data formatting | bytes 393216

commit v6 on v4

--- a/solution.py
+++ b/solution.py
@@ -158,15 +158,11 @@
         reply[step, b, h] = mm(full_t[b], vec[step, h]).astype(BF16)
         reply_copy(step, b, h).start()
 
-    loads[1].wait()
-    pl.semaphore_wait(barrier, neighbours)
-    send_vectors(0, 0)
-
     for table in tables:
         table.wait()
     flips = [jnp.bitwise_xor(matchings[m, group], group) for m in range(matches)]
     loads[0].wait()
-    for b in order:
+    for at, b in enumerate(order):
         hits = [jnp.where(flips[m] == (1 << b), 1, 0) for m in range(matches)]
         which = jnp.minimum(sum(m * hits[m] for m in range(matches)), matches - 1)
         present = sum(hits)
@@ -177,11 +173,14 @@
                 block = pair_raw[which, pl.ds(i * BLK, BLK), pl.ds(j * BLK, BLK)]
                 own[b, pl.ds(i * BLK, BLK), pl.ds(j * BLK, BLK)] = block * keep
 
+        if at == 0:
+            pl.semaphore_wait(barrier, neighbours)
+
         @pl.when(gives[b])
         def _():
             block_copy(b).start()
 
-    for h in range(1, halves):
+    for h in range(halves):
         loads[1 + h].wait()
         send_down(0, h)
 
@@ -233,14 +232,19 @@
             send_reply(0, b, 0)
 
         if b == 0:
-            for c in order:
+            for c in range(bits):
                 @pl.when(gives[c])
                 def _():
                     block_copy(c).wait_send()
-                    for h in range(1, halves):
-                        given_copy(0, c, h).start()
+                    given_copy(0, c, 0).start()
 
     for h in range(1, halves):
+        for b in range(bits):
+            @pl.when(gives[b])
+            def _():
+                given_copy(0, b, h - 1).wait_send()
+                given_copy(0, b, h).start()
+
         for b in order:
             @pl.when(holds[b])
             def _():
@@ -296,9 +300,9 @@
     for b in range(bits):
         @pl.when(gives[b])
         def _():
-            for step in range(2):
-                for h in range(halves):
-                    given_copy(step, b, h).wait_send()
+            given_copy(0, b, halves - 1).wait_send()
+            for h in range(halves):
+                given_copy(1, b, h).wait_send()
 
         @pl.when(holds[b])
         def _():

time: 32.7 us -> 31.3 us (0.957)
  Pallas kernels: 31.9 us -> 30.5 us
    pallas_call x1, Pallas kernels: 31.9 us -> 30.5 us  [on_device(): pl.pallas_call(functools.partial(filter_kernel, bits, shells), out_shape=...]
where the time goes in v6:
time: 31.3 us; the launch traced here: 31.2 us
  Pallas kernels  30.5 us (97%)
  local copies, waits for them, and re-layouts  0.68 us (2%)
    pallas_call x1, Pallas kernels, on_device(): pl.pallas_call(functools.partial(filter_kernel, bits, shells), out_shape=...  30.5 us
    unnamed x1, local copies, waits for them, and re-layouts  0.68 us

profile of v6, /device:TPU:0, one launch (start us, length us, event | category | flops | bytes accessed | tf_op | source)
XLA Modules:
  0.0 31.2 jit_solution(251594171697998826)
XLA Ops:
  0.0 30.5 %shard_map.73 = bf16[384,256]{1,0:T(8,128)(2,1)S(1)} custom-call(bf16[384,256]{1,0:T(8,128)(2,1)} %bitcast.11, bf16[384,384]{1,0:T(8,128)(2,1)} %bitcast.9, bf16[3,384,384]{2,1,0:T(8,128)(2,1)} %bitcast.8, bf16[384,384]{1,0:T(8,128)(2,1)} %bitcast.10, s32[9,1,3]{2,1,0:T(1,128)} %bitcast.12, s32[3,1,3]{2,1,0:T(1,128)} %bitcast.13, s32[3,8]{1,0:T(4,128)} %matchings_hbm.1), custom_call_target="tpu_custom_call" | custom-call | tf_op jit(solution)/shard_map/pallas_call | solution.py:335
  30.5 0.7 %copy.15 = bf16[1,1,384,256]{3,2,1,0:T(8,128)(2,1)} copy(bf16[1,1,384,256]{3,2,1,0:T(8,128)(2,1)S(1)} %bitcast.7) | data formatting | bytes 393216

commit v7 on v3

--- a/solution.py
+++ b/solution.py
@@ -20,6 +20,10 @@
 
 def mm(a, b):
     return jnp.dot(a, b, preferred_element_type=F32)
+
+
+def mm_t(a, b):
+    return lax.dot_general(a, b, (((1,), (1,)), ((), ())), preferred_element_type=F32)
 
 
 def turned(x):
@@ -40,17 +44,15 @@
     pair_mask,
     shell_mask,
     matchings,
+    vec_raw,
     vec,
     local_raw,
     pair_raw,
     shell_raw,
     own,
     theirs,
-    full,
-    full_t,
-    sym,
     up,
-    up_t,
+    partial,
     reply,
     arrived,
     lift,
@@ -67,7 +69,7 @@
     rise_send,
     rise_recv,
 ):
-    halves = vec.shape[1]
+    halves = vec.shape[1] // LANES
     rows = vec.shape[2]
     parts = rows // BLK
     matches = pair_raw.shape[0]
@@ -81,14 +83,15 @@
         return (group // (1 << b)) % 2
 
     partner = [group + (1 << b) - 2 * (1 << b) * digit(b) for b in range(bits)]
-    role = [(digit(b) + (digit((b + 1) % bits) if bits > 1 else 0) + shell) % 2 for b in range(bits)]
+    other = [bits - 1] + [(b + 1) % bits for b in range(1, bits)]
+    role = [(digit(b) + (digit(other[b]) if bits > 1 else 0) + (b == 0) + shell) % 2 for b in range(bits)]
     holds = [role[b] == 1 for b in range(bits)]
     gives = [role[b] == 0 for b in range(bits)]
 
     columns = lambda h: pl.ds(h * LANES, LANES)
     loads = [pltpu.make_async_copy(pair_hbm, pair_raw, load_sem.at[0])]
     for h in range(halves):
-        loads.append(pltpu.make_async_copy(vec_hbm.at[:, columns(h)], vec.at[0, h], load_sem.at[1 + h]))
+        loads.append(pltpu.make_async_copy(vec_hbm.at[:, columns(h)], vec_raw.at[:, columns(h)], load_sem.at[1 + h]))
     loads.append(pltpu.make_async_copy(shell_hbm, shell_raw, load_sem.at[1 + halves]))
     loads.append(pltpu.make_async_copy(local_hbm, local_raw, load_sem.at[2 + halves]))
     tables = [
@@ -106,23 +109,23 @@
 
     def edge_copy(source, step, b, h):
         return pltpu.make_async_remote_copy(
-            src_ref=source, dst_ref=arrived.at[step, b, h], send_sem=edge_send.at[step, b, h],
+            src_ref=source, dst_ref=arrived.at[step, b, columns(h)], send_sem=edge_send.at[step, b, h],
             recv_sem=edge_recv.at[step, b, h], device_id={"grp": partner[b]}, device_id_type=MESH)
 
     def given_copy(step, b, h):
-        return edge_copy(vec.at[step, h], step, b, h)
+        return edge_copy(vec.at[step, columns(h)], step, b, h)
 
     def reply_copy(step, b, h):
-        return edge_copy(reply.at[step, b, h], step, b, h)
+        return edge_copy(reply.at[step, b, columns(h)], step, b, h)
 
     def down_copy(step, h):
         return pltpu.make_async_remote_copy(
-            src_ref=vec.at[step, h], dst_ref=from_up.at[step, h], send_sem=down_send.at[step, h],
+            src_ref=vec.at[step, columns(h)], dst_ref=from_up.at[step, columns(h)], send_sem=down_send.at[step, h],
             recv_sem=down_recv.at[step, h], device_id={"shell": shell - 1}, device_id_type=MESH)
 
     def rise_copy(step, h):
         return pltpu.make_async_remote_copy(
-            src_ref=lift.at[step, h], dst_ref=from_down.at[step, h], send_sem=rise_send.at[step, h],
+            src_ref=lift.at[step, columns(h)], dst_ref=from_down.at[step, columns(h)], send_sem=rise_send.at[step, h],
             recv_sem=rise_recv.at[step, h], device_id={"shell": shell + 1}, device_id_type=MESH)
 
     barrier = pltpu.get_barrier_semaphore()
@@ -169,19 +172,28 @@
         def _():
             down_copy(step, h).start()
 
-    def send_lift(step, h):
+    def start_lift(step, h):
         @pl.when(has_up)
         def _():
-            lift[step, h] = mm(up_t[...], vec[step, h]).astype(BF16)
             rise_copy(step, h).start()
 
-    def send_reply(step, b, h):
-        reply[step, b, h] = mm(full_t[b], vec[step, h]).astype(BF16)
-        reply_copy(step, b, h).start()
+    def start_replies(step, h):
+        for b in order:
+            @pl.when(holds[b])
+            def _():
+                reply_copy(step, b, h).start()
 
     for h in range(halves):
         loads[1 + h].wait()
+        for i in range(parts):
+            here = pl.ds(i * BLK, BLK)
+            vec[0, columns(h), here] = turned(vec_raw[here, columns(h)]).astype(BF16)
         send_vectors(0, h)
+
+    for b in range(bits):
+        @pl.when(holds[b])
+        def _():
+            partial[b] = mm(vec[0], own[b])
 
     loads[1 + halves].wait()
     for i in range(parts):
@@ -189,99 +201,83 @@
             keep = shell_mask[i, 0, j].astype(F32)
             block = shell_raw[pl.ds(i * BLK, BLK), pl.ds(j * BLK, BLK)].astype(F32) * keep
             up[pl.ds(i * BLK, BLK), pl.ds(j * BLK, BLK)] = block.astype(BF16)
-            up_t[pl.ds(j * BLK, BLK), pl.ds(i * BLK, BLK)] = block.T.astype(BF16)
-    for h in range(halves):
-        send_lift(0, h)
+
+    @pl.when(has_up)
+    def _():
+        lift[0] = mm(vec[0], up[...]).astype(BF16)
+
+    for h in range(halves):
+        start_lift(0, h)
 
     loads[2 + halves].wait()
-    for i in range(parts):
-        for j in range(parts):
-            here, there = pl.ds(i * BLK, BLK), pl.ds(j * BLK, BLK)
-            sym[here, there] = (local_raw[here, there].astype(F32) + turned(local_raw[there, here])).astype(BF16)
-
-    def begin(step, h):
-        v = vec[step, h]
-        acc[step, h] = mm(sym[...], v) - spectrum_center * v.astype(F32)
-
-    for h in range(halves):
-        begin(0, h)
-
-    def each_block(work):
-        for i in range(parts):
-            for j in range(parts):
-                work(pl.ds(i * BLK, BLK), pl.ds(j * BLK, BLK))
+
+    def begin(step, part):
+        v = vec[step, part]
+        acc[step, part] = mm_t(v, local_raw[...]) + mm(v, local_raw[...]) - spectrum_center * v.astype(F32)
+
+    begin(0, pl.ds(0, halves * LANES))
 
     for b in range(bits):
         @pl.when(holds[b])
         def _():
-            def turn(here, there):
-                full_t[b, here, there] = turned(own[b, there, here]).astype(BF16)
-
-            each_block(turn)
-
-    for b in range(bits):
-        @pl.when(holds[b])
-        def _():
-            def join(here, there):
-                k_t = theirs[b, here, there].astype(F32) + full_t[b, here, there].astype(F32)
-                full_t[b, here, there] = k_t.astype(BF16)
-
             block_copy(b).wait_recv()
-            each_block(join)
-            send_reply(0, b, 0)
+            reply[0, b] = (partial[b] + mm_t(vec[0], theirs[b])).astype(BF16)
+            reply_copy(0, b, 0).start()
 
     for h in range(1, halves):
-        for b in order:
+        start_replies(0, h)
+
+    def gather(step, h):
+        part = columns(h)
+
+        @pl.when(has_up)
+        def _():
+            down_copy(step, h).wait_recv()
+            acc[step, part] += mm_t(from_up[step, part], up[...])
+
+        @pl.when(has_down)
+        def _():
+            rise_copy(step, h).wait_recv()
+            acc[step, part] += from_down[step, part].astype(F32)
+
+        for b in range(bits):
             @pl.when(holds[b])
             def _():
-                send_reply(0, b, h)
-
-    for b in range(bits):
-        @pl.when(holds[b])
-        def _():
-            def turn_back(here, there):
-                full[b, there, here] = turned(full_t[b, here, there]).astype(BF16)
-
-            each_block(turn_back)
-
-    def gather(step, h):
-        @pl.when(has_up)
-        def _():
-            down_copy(step, h).wait_recv()
-            acc[step, h] += mm(up[...], from_up[step, h])
-
-        @pl.when(has_down)
-        def _():
-            rise_copy(step, h).wait_recv()
-            acc[step, h] += from_down[step, h].astype(F32)
-
-        for b in reversed(order):
-            @pl.when(holds[b])
-            def _():
                 given_copy(step, b, h).wait_recv()
-                acc[step, h] += mm(full[b], arrived[step, b, h])
-
-        for b in reversed(order):
+                x = arrived[step, b, part]
+                acc[step, part] += mm_t(x, own[b]) + mm(x, theirs[b])
+
+        for b in range(bits):
             @pl.when(gives[b])
             def _():
                 reply_copy(step, b, h).wait_recv()
-                acc[step, h] += arrived[step, b, h].astype(F32)
-
-    for h in range(halves):
+                acc[step, part] += arrived[step, b, part].astype(F32)
+
+    for h in range(halves):
+        part = columns(h)
         gather(0, h)
-        vec[1, h] = (acc[0, h] * (1.0 / spectrum_halfwidth)).astype(BF16)
+        vec[1, part] = (acc[0, part] * (1.0 / spectrum_halfwidth)).astype(BF16)
         send_vectors(1, h)
         for b in order:
             @pl.when(holds[b])
             def _():
-                send_reply(1, b, h)
-        send_lift(1, h)
-        begin(1, h)
+                v = vec[1, part]
+                reply[1, b, part] = (mm(v, own[b]) + mm_t(v, theirs[b])).astype(BF16)
+                reply_copy(1, b, h).start()
+
+        @pl.when(has_up)
+        def _():
+            lift[1, part] = mm(vec[1, part], up[...]).astype(BF16)
+
+        start_lift(1, h)
+        begin(1, part)
 
     for h in range(halves):
         gather(1, h)
-        y2 = acc[1, h] * (2.0 / spectrum_halfwidth) - vec[0, h].astype(F32)
-        out[:, columns(h)] = y2.astype(BF16)
+        for i in range(parts):
+            here = pl.ds(i * BLK, BLK)
+            y2 = (acc[1, columns(h), here] * (2.0 / spectrum_halfwidth)).T - vec_raw[here, columns(h)].astype(F32)
+            out[here, columns(h)] = y2.astype(BF16)
 
     for b in range(bits):
         @pl.when(gives[b])
@@ -318,7 +314,7 @@
     pair_masks = pair_masks.reshape(matches * parts, 1, parts)
     shell_mask = shell_mask.reshape(parts, 1, parts)
     square = (rows, rows)
-    tall = (halves, rows, LANES)
+    wide = (width, rows)
     out = pl.pallas_call(
         functools.partial(filter_kernel, bits, shells),
         out_shape=jax.ShapeDtypeStruct((rows, width), BF16),
@@ -328,23 +324,21 @@
             pltpu.SMEM(pair_masks.shape, jnp.int32),
             pltpu.SMEM(shell_mask.shape, jnp.int32),
             pltpu.SMEM(matchings.shape, jnp.int32),
-            pltpu.VMEM((2,) + tall, BF16),
+            pltpu.VMEM((rows, width), BF16),
+            pltpu.VMEM((2,) + wide, BF16),
             pltpu.VMEM(square, BF16),
             pltpu.VMEM((matches,) + square, BF16),
             pltpu.VMEM(square, BF16),
             pltpu.VMEM((bits,) + square, BF16),
             pltpu.VMEM((bits,) + square, BF16),
-            pltpu.VMEM((bits,) + square, BF16),
-            pltpu.VMEM((bits,) + square, BF16),
             pltpu.VMEM(square, BF16),
-            pltpu.VMEM(square, BF16),
-            pltpu.VMEM(square, BF16),
-            pltpu.VMEM((2, bits) + tall, BF16),
-            pltpu.VMEM((2, bits) + tall, BF16),
-            pltpu.VMEM((2,) + tall, BF16),
-            pltpu.VMEM((2,) + tall, BF16),
-            pltpu.VMEM((2,) + tall, BF16),
-            pltpu.VMEM((2,) + tall, F32),
+            pltpu.VMEM((bits,) + wide, F32),
+            pltpu.VMEM((2, bits) + wide, BF16),
+            pltpu.VMEM((2, bits) + wide, BF16),
+            pltpu.VMEM((2,) + wide, BF16),
+            pltpu.VMEM((2,) + wide, BF16),
+            pltpu.VMEM((2,) + wide, BF16),
+            pltpu.VMEM((2,) + wide, F32),
             pltpu.SemaphoreType.DMA((6 + halves,)),
             pltpu.SemaphoreType.DMA((bits,)),
             pltpu.SemaphoreType.DMA((bits,)),

time: 30.6 us -> 31 us (1.013)
  Pallas kernels: 29.7 us -> 30.1 us
    pallas_call x1, Pallas kernels: 29.7 us -> 30.1 us  [on_device(): pl.pallas_call(functools.partial(filter_kernel, bits, shells), out_shape=...]
where the time goes in v7:
time: 31 us; the launch traced here: 30.8 us
  Pallas kernels  30.1 us (97%)
  local copies, waits for them, and re-layouts  0.68 us (2%)
    pallas_call x1, Pallas kernels, on_device(): pl.pallas_call(functools.partial(filter_kernel, bits, shells), out_shape=...  30.1 us
    unnamed x1, local copies, waits for them, and re-layouts  0.68 us

profile of v7, /device:TPU:0, one launch (start us, length us, event | category | flops | bytes accessed | tf_op | source)
XLA Modules:
  0.0 30.8 jit_solution(18392684776325049320)
XLA Ops:
  0.0 30.1 %shard_map.73 = bf16[384,256]{1,0:T(8,128)(2,1)S(1)} custom-call(bf16[384,256]{1,0:T(8,128)(2,1)} %bitcast.11, bf16[384,384]{1,0:T(8,128)(2,1)} %bitcast.9, bf16[3,384,384]{2,1,0:T(8,128)(2,1)} %bitcast.8, bf16[384,384]{1,0:T(8,128)(2,1)} %bitcast.10, s32[9,1,3]{2,1,0:T(1,128)} %bitcast.12, s32[3,1,3]{2,1,0:T(1,128)} %bitcast.13, s32[3,8]{1,0:T(4,128)} %matchings_hbm.1), custom_call_target="tpu_custom_call" | custom-call | tf_op jit(solution)/shard_map/pallas_call | solution.py:318
  30.1 0.7 %copy.15 = bf16[1,1,384,256]{3,2,1,0:T(8,128)(2,1)} copy(bf16[1,1,384,256]{3,2,1,0:T(8,128)(2,1)S(1)} %bitcast.7) | data formatting | bytes 393216

commit v8 on v7

--- a/solution.py
+++ b/solution.py
@@ -162,33 +162,30 @@
         def _():
             block_copy(b).start()
 
+    def send_down(step, h):
+        @pl.when(has_down)
+        def _():
+            down_copy(step, h).start()
+
     def send_vectors(step, h):
         for b in order:
             @pl.when(gives[b])
             def _():
                 given_copy(step, b, h).start()
 
-        @pl.when(has_down)
-        def _():
-            down_copy(step, h).start()
+        send_down(step, h)
 
     def start_lift(step, h):
         @pl.when(has_up)
         def _():
             rise_copy(step, h).start()
-
-    def start_replies(step, h):
-        for b in order:
-            @pl.when(holds[b])
-            def _():
-                reply_copy(step, b, h).start()
 
     for h in range(halves):
         loads[1 + h].wait()
         for i in range(parts):
             here = pl.ds(i * BLK, BLK)
             vec[0, columns(h), here] = turned(vec_raw[here, columns(h)]).astype(BF16)
-        send_vectors(0, h)
+        send_down(0, h)
 
     for b in range(bits):
         @pl.when(holds[b])
@@ -224,8 +221,24 @@
             reply[0, b] = (partial[b] + mm_t(vec[0], theirs[b])).astype(BF16)
             reply_copy(0, b, 0).start()
 
+        if b == 0:
+            for c in range(bits):
+                @pl.when(gives[c])
+                def _():
+                    block_copy(c).wait_send()
+                    given_copy(0, c, 0).start()
+
     for h in range(1, halves):
-        start_replies(0, h)
+        for b in range(bits):
+            @pl.when(gives[b])
+            def _():
+                given_copy(0, b, h - 1).wait_send()
+                given_copy(0, b, h).start()
+
+            @pl.when(holds[b])
+            def _():
+                reply_copy(0, b, h - 1).wait_send()
+                reply_copy(0, b, h).start()
 
     def gather(step, h):
         part = columns(h)
@@ -282,16 +295,15 @@
     for b in range(bits):
         @pl.when(gives[b])
         def _():
-            block_copy(b).wait_send()
-            for step in range(2):
-                for h in range(halves):
-                    given_copy(step, b, h).wait_send()
+            given_copy(0, b, halves - 1).wait_send()
+            for h in range(halves):
+                given_copy(1, b, h).wait_send()
 
         @pl.when(holds[b])
         def _():
-            for step in range(2):
-                for h in range(halves):
-                    reply_copy(step, b, h).wait_send()
+            reply_copy(0, b, halves - 1).wait_send()
+            for h in range(halves):
+                reply_copy(1, b, h).wait_send()
 
     @pl.when(has_down)
     def _():

time: 31 us -> 32.8 us (1.058)
  Pallas kernels: 30.1 us -> 31.9 us
    pallas_call x1, Pallas kernels: 30.1 us -> 31.9 us  [on_device(): pl.pallas_call(functools.partial(filter_kernel, bits, shells), out_shape=...]
where the time goes in v8:
time: 32.8 us; the launch traced here: 32.6 us
  Pallas kernels  31.9 us (97%)
  local copies, waits for them, and re-layouts  0.68 us (2%)
    pallas_call x1, Pallas kernels, on_device(): pl.pallas_call(functools.partial(filter_kernel, bits, shells), out_shape=...  31.9 us
    unnamed x1, local copies, waits for them, and re-layouts  0.68 us

profile of v8, /device:TPU:0, one launch (start us, length us, event | category | flops | bytes accessed | tf_op | source)
XLA Modules:
  0.0 32.6 jit_solution(12587662091360642903)
XLA Ops:
  0.0 31.9 %shard_map.73 = bf16[384,256]{1,0:T(8,128)(2,1)S(1)} custom-call(bf16[384,256]{1,0:T(8,128)(2,1)} %bitcast.11, bf16[384,384]{1,0:T(8,128)(2,1)} %bitcast.9, bf16[3,384,384]{2,1,0:T(8,128)(2,1)} %bitcast.8, bf16[384,384]{1,0:T(8,128)(2,1)} %bitcast.10, s32[9,1,3]{2,1,0:T(1,128)} %bitcast.12, s32[3,1,3]{2,1,0:T(1,128)} %bitcast.13, s32[3,8]{1,0:T(4,128)} %matchings_hbm.1), custom_call_target="tpu_custom_call" | custom-call | tf_op jit(solution)/shard_map/pallas_call | solution.py:330
  31.9 0.7 %copy.15 = bf16[1,1,384,256]{3,2,1,0:T(8,128)(2,1)} copy(bf16[1,1,384,256]{3,2,1,0:T(8,128)(2,1)S(1)} %bitcast.7) | data formatting | bytes 393216

commit v9 on v8

--- a/solution.py
+++ b/solution.py
@@ -185,7 +185,10 @@
         for i in range(parts):
             here = pl.ds(i * BLK, BLK)
             vec[0, columns(h), here] = turned(vec_raw[here, columns(h)]).astype(BF16)
-        send_down(0, h)
+        if h == 0:
+            send_vectors(0, h)
+        else:
+            send_down(0, h)
 
     for b in range(bits):
         @pl.when(holds[b])
@@ -226,15 +229,11 @@
                 @pl.when(gives[c])
                 def _():
                     block_copy(c).wait_send()
-                    given_copy(0, c, 0).start()
+                    for h in range(1, halves):
+                        given_copy(0, c, h).start()
 
     for h in range(1, halves):
         for b in range(bits):
-            @pl.when(gives[b])
-            def _():
-                given_copy(0, b, h - 1).wait_send()
-                given_copy(0, b, h).start()
-
             @pl.when(holds[b])
             def _():
                 reply_copy(0, b, h - 1).wait_send()
@@ -295,9 +294,9 @@
     for b in range(bits):
         @pl.when(gives[b])
         def _():
-            given_copy(0, b, halves - 1).wait_send()
-            for h in range(halves):
-                given_copy(1, b, h).wait_send()
+            for step in range(2):
+                for h in range(halves):
+                    given_copy(step, b, h).wait_send()
 
         @pl.when(holds[b])
         def _():

time: 32.8 us -> 32.9 us (level)
  no operation moved by 1% of the time
where the time goes in v9:
time: 32.9 us; the launch traced here: 32.8 us
  Pallas kernels  32.1 us (98%)
  local copies, waits for them, and re-layouts  0.68 us (2%)
    pallas_call x1, Pallas kernels, on_device(): pl.pallas_call(functools.partial(filter_kernel, bits, shells), out_shape=...  32.1 us
    unnamed x1, local copies, waits for them, and re-layouts  0.68 us

profile of v9, /device:TPU:0, one launch (start us, length us, event | category | flops | bytes accessed | tf_op | source)
XLA Modules:
  0.0 32.8 jit_solution(2286037450648478549)
XLA Ops:
  0.0 32.1 %shard_map.73 = bf16[384,256]{1,0:T(8,128)(2,1)S(1)} custom-call(bf16[384,256]{1,0:T(8,128)(2,1)} %bitcast.11, bf16[384,384]{1,0:T(8,128)(2,1)} %bitcast.9, bf16[3,384,384]{2,1,0:T(8,128)(2,1)} %bitcast.8, bf16[384,384]{1,0:T(8,128)(2,1)} %bitcast.10, s32[9,1,3]{2,1,0:T(1,128)} %bitcast.12, s32[3,1,3]{2,1,0:T(1,128)} %bitcast.13, s32[3,8]{1,0:T(4,128)} %matchings_hbm.1), custom_call_target="tpu_custom_call" | custom-call | tf_op jit(solution)/shard_map/pallas_call | solution.py:329
  32.1 0.7 %copy.15 = bf16[1,1,384,256]{3,2,1,0:T(8,128)(2,1)} copy(bf16[1,1,384,256]{3,2,1,0:T(8,128)(2,1)S(1)} %bitcast.7) | data formatting | bytes 393216

commit v10 on v7

--- a/solution.py
+++ b/solution.py
@@ -177,12 +177,6 @@
         def _():
             rise_copy(step, h).start()
 
-    def start_replies(step, h):
-        for b in order:
-            @pl.when(holds[b])
-            def _():
-                reply_copy(step, b, h).start()
-
     for h in range(halves):
         loads[1 + h].wait()
         for i in range(parts):
@@ -222,10 +216,8 @@
         def _():
             block_copy(b).wait_recv()
             reply[0, b] = (partial[b] + mm_t(vec[0], theirs[b])).astype(BF16)
-            reply_copy(0, b, 0).start()
-
-    for h in range(1, halves):
-        start_replies(0, h)
+            for h in range(halves):
+                reply_copy(0, b, h).start()
 
     def gather(step, h):
         part = columns(h)

time: 31 us -> 30.8 us (level)
  no operation moved by 1% of the time
where the time goes in v10:
time: 30.8 us; the launch traced here: 30.6 us
  Pallas kernels  29.9 us (97%)
  local copies, waits for them, and re-layouts  0.68 us (2%)
    pallas_call x1, Pallas kernels, on_device(): pl.pallas_call(functools.partial(filter_kernel, bits, shells), out_shape=...  29.9 us
    unnamed x1, local copies, waits for them, and re-layouts  0.68 us

profile of v10, /device:TPU:0, one launch (start us, length us, event | category | flops | bytes accessed | tf_op | source)
XLA Modules:
  0.0 30.6 jit_solution(10116035790488767434)
XLA Ops:
  0.0 29.9 %shard_map.73 = bf16[384,256]{1,0:T(8,128)(2,1)S(1)} custom-call(bf16[384,256]{1,0:T(8,128)(2,1)} %bitcast.11, bf16[384,384]{1,0:T(8,128)(2,1)} %bitcast.9, bf16[3,384,384]{2,1,0:T(8,128)(2,1)} %bitcast.8, bf16[384,384]{1,0:T(8,128)(2,1)} %bitcast.10, s32[9,1,3]{2,1,0:T(1,128)} %bitcast.12, s32[3,1,3]{2,1,0:T(1,128)} %bitcast.13, s32[3,8]{1,0:T(4,128)} %matchings_hbm.1), custom_call_target="tpu_custom_call" | custom-call | tf_op jit(solution)/shard_map/pallas_call | solution.py:310
  29.9 0.7 %copy.15 = bf16[1,1,384,256]{3,2,1,0:T(8,128)(2,1)} copy(bf16[1,1,384,256]{3,2,1,0:T(8,128)(2,1)S(1)} %bitcast.7) | data formatting | bytes 393216
